TPU v7x, 32 devices: a whole 2x2x4 slice. The times are simulated.
32 devices in a mesh: scenes: 2 (over y), rows: 4 (over x, core), cols: 4 (over z).
Axes of the slice: x: 2, y: 2, z: 4, core: 2. Of those that a mesh axis runs over, the one named last changes fastest.
Arguments:
- features: bfloat16 [256, 64, 256], P(('scenes', 'rows'), 'cols'), parts along dimension 0, may hold values from -100 to 100
- dw_kernel: bfloat16 [7, 7, 256], replicated, may hold values from -0.875 to 0.875
- norm_gain: float32 [256], replicated, may hold values from 0.1 to 1.9
- query_state: bfloat16 [600, 256], P('scenes'), parts along dimension 0, may hold values from -6 to 6
- query_pos: bfloat16 [600, 256], P('scenes'), parts along dimension 0, may hold values from -175 to 175
- w_query: bfloat16 [256, 256], replicated, may hold values from -0.375 to 0.375
- w_key: bfloat16 [256, 256], replicated, may hold values from -0.375 to 0.375
- w_value: bfloat16 [256, 256], replicated, may hold values from -0.375 to 0.375
- w_out: bfloat16 [256, 256], replicated, may hold values from -0.375 to 0.375
Outputs:
- memory: bfloat16 [256, 64, 256], P(('scenes', 'rows'), 'cols'), parts along dimension 0
- decoded: float32 [600, 256], P('scenes'), parts along dimension 0
There are 2 independent parts, one for each index of `scenes`. A program takes and returns all parts, laid end to end along the dimension named above; an argument that names none is the same for every part. Nothing has to cross between parts.
All inputs are finite; a program needn't handle non-finite values.
Results may differ from a plain program's by a relative error of at most 0.0024.
The roundings to bfloat16 on the way count: a program that leaves them out, or rounds other values in their place, can miss the bound.
Values may be sent and summed in bfloat16 or wider, within the bound.
A program may use at most 64 MiB of HBM per device.

v0:
```python
import jax
import jax.numpy as jnp
from jax import lax
from jax.sharding import PartitionSpec as P

HEADS = 8


def with_halo(value, sides, width):
    for axis, dim in sides:
        size, length = (lax.axis_size(axis), value.shape[dim])
        up = [(i, (i + 1) % size) for i in range(size - 1)]
        down = [(j, i) for i, j in up]
        last = lax.slice_in_dim(value, length - width, length, axis=dim)
        initial = lax.slice_in_dim(value, 0, width, axis=dim)
        before = lax.ppermute(last, axis, up)
        after = lax.ppermute(initial, axis, down)
        value = jnp.concatenate([before, value, after], axis=dim)
    return value


def layer_norm(vector):
    centred = vector - jnp.mean(vector, axis=-1, keepdims=True)
    variance = jnp.mean(centred * centred, axis=-1, keepdims=True)
    return centred * lax.rsqrt(variance + 1e-06)


def body(features, dw_kernel, norm_gain, query_state, query_pos, w_query, w_key, w_value, w_out):
    tile_rows, tile_cols, width = features.shape
    head_dim = width // HEADS
    row_padded = with_halo(features, (("rows", 0),), 3)
    padded = with_halo(row_padded, (("cols", 1),), 3)
    kernel = dw_kernel.astype(jnp.float32)
    conv = jnp.zeros((tile_rows, tile_cols, width), jnp.float32)
    for offset_row in range(7):
        for offset_col in range(7):
            window = padded[
                offset_row : offset_row + tile_rows, offset_col : offset_col + tile_cols, :
            ]
            conv = conv + window.astype(jnp.float32) * kernel[offset_row, offset_col]
    memory = (features.astype(jnp.float32) + layer_norm(conv) * norm_gain).astype(jnp.bfloat16)
    flat = memory.reshape(tile_rows * tile_cols, width)
    keys = jnp.dot(flat, w_key, preferred_element_type=jnp.float32).astype(jnp.bfloat16)
    values = jnp.dot(flat, w_value, preferred_element_type=jnp.float32).astype(jnp.bfloat16)
    mixed = (query_state.astype(jnp.float32) + query_pos.astype(jnp.float32)).astype(jnp.bfloat16)
    queries = (
        jnp.dot(mixed, w_query, preferred_element_type=jnp.float32) * head_dim ** (-0.5)
    ).astype(jnp.bfloat16)
    max_list = []
    total_list = []
    sum_list = []
    for head_index in range(HEADS):
        low = head_index * head_dim
        scores = lax.dot_general(
            queries[:, low : low + head_dim],
            keys[:, low : low + head_dim],
            (((1,), (1,)), ((), ())),
            preferred_element_type=jnp.float32,
        )
        local_max = jnp.max(scores, axis=-1)
        expo = jnp.exp(scores - local_max[:, None])
        total_list.append(jnp.sum(expo, axis=-1))
        max_list.append(local_max)
        sum_list.append(
            jnp.dot(
                expo.astype(jnp.bfloat16),
                values[:, low : low + head_dim],
                preferred_element_type=jnp.float32,
            )
        )
    maxima = jnp.stack(max_list, axis=1)
    totals = jnp.stack(total_list, axis=1)
    sums = jnp.concatenate(sum_list, axis=1)

    def widen(factor):
        return jnp.repeat(factor, head_dim, axis=1)

    global_max = lax.pmax(maxima, ("rows", "cols"))
    rescale = jnp.exp(maxima - global_max)
    totals, sums = lax.psum((totals * rescale, sums * widen(rescale)), ("rows", "cols"))
    attended = (sums / widen(totals)).astype(jnp.bfloat16)
    projected = jnp.dot(attended, w_out, preferred_element_type=jnp.float32)
    decoded = layer_norm(query_state.astype(jnp.float32) + projected)
    return (memory, decoded)


def solution(mesh):
    in_specs = (
        P(("scenes", "rows"), "cols", None),
        P(),
        P(),
        P("scenes", None),
        P("scenes", None),
        P(),
        P(),
        P(),
        P(),
    )
    out_specs = (P(("scenes", "rows"), "cols", None), P("scenes", None))
    return jax.shard_map(body, mesh=mesh, in_specs=in_specs, out_specs=out_specs, check_vma=False)
```

profile of v0, /device:TPU:0, one launch (start us, length us, event | category | flops | bytes accessed | tf_op | source)
XLA Modules:
  0.0 220.0 jit_solution(14849400195409667426)
XLA Ops:
  7.2 0.8 fusion.138
  8.0 2.3 %collective-permute-start = (bf16[3,16,256]{2,1,0:T(8,128)(2,1)S(1)}, bf16[3,16,256]{2,1,0:T(8,128)(2,1)S(1)}, u32[]{:S(2)}, u32[]{:S(2)}) collective-permute-start(bf16[3,16,256]{2,1,0:T(8,128)(2,1)S(1)} %get-tuple-element.12), channel_id=1, source_target_pairs={{0,4},{4,8},{8,12},{1,5},{5,9},{9,13},{2,6},{6,10},{10,14},{3,7},{... | collective-permute-start | bytes 73736 | tf_op jit(solution)/shard_map/ppermute | solution.py:16
  10.4 1.3 collective-permute-start.1
  11.7 1.0 fusion.139
  12.7 1.2 fusion
  14.1 1.5 collective-permute-done.1
  15.7 3.5 %collective-permute-start.2 = (bf16[38,3,256]{2,1,0:T(4,128)(2,1)S(1)}, bf16[38,3,256]{2,1,0:T(4,128)(2,1)S(1)}, u32[]{:S(2)}, u32[]{:S(2)}) collective-permute-start(bf16[38,3,256]{2,1,0:T(4,128)(2,1)S(1)} %get-tuple-element.6), channel_id=1, source_target_pairs={{0,1},{1,2},{2,3},{4,5},{5,6},{6,7},{8,9},{9,10},{10,11},{12,13},{... | collective-permute-start | bytes 175112 | tf_op jit(solution)/shard_map/ppermute | solution.py:16
  19.1 1.3 collective-permute-start.3
  20.5 0.7 collective-permute-done.2
  21.1 4.3 %collective-permute-done.3 = bf16[38,3,256]{2,1,0:T(4,128)(2,1)S(1)} collective-permute-done((bf16[38,3,256]{2,1,0:T(4,128)(2,1)S(1)}, bf16[38,3,256]{2,1,0:T(4,128)(2,1)S(1)}, u32[]{:S(2)}, u32[]{:S(2)}) %collective-permute-start.3) | collective-permute-done | bytes 58400 | tf_op jit(solution)/shard_map/ppermute | solution.py:17
  25.4 6.2 %fusion.135 = (f32[32,16]{1,0:T(8,128)S(1)}, f32[32,16,256]{2,1,0:T(8,128)S(1)}) fusion(f32[256]{0:T(256)S(1)} %bitcast.113, bf16[38,3,256]{2,1,0:T(4,128)(2,1)S(1)} %collective-permute-done.3, bf16[38,16,256]{2,1,0:T(8,128)(2,1)S(1)} %get-tuple-element.65, f32[256]{0:T(256)S(1)} %bitcast.112, f32[256]{0:T(256)S(1)} %bitcast.111, f32[256]{0:T(256)S(1)} %bitcast.110, ...), kind=kLoop, calls=%fused_computation.248 | loop fusion | flops 35782144 | bytes 2839552 | tf_op jit(solution)/shard_map/reduce_sum | solution.py:23
  31.9 0.7 copy-done.23
  33.1 1.0 fusion.142
  34.1 1.1 fusion.143
  35.2 1.1 fusion.144
  37.1 0.4 fusion.147
  37.4 0.4 fusion.148
  38.3 0.6 broadcast_in_dim.38
  38.8 0.6 broadcast_in_dim.39
  39.4 0.6 broadcast_in_dim.40
  40.0 0.6 broadcast_in_dim.41
  40.6 0.6 broadcast_in_dim.42
  41.2 0.7 stack.38
  41.9 59.7 %pmax.7 = f32[300,8]{0,1:T(8,128)S(1)} all-reduce(f32[300,8]{0,1:T(8,128)S(1)} %stack.38), channel_id=1, replica_groups=mesh['scenes'=2,'rows'=4,'cols'=4] {'rows','cols'}, use_global_device_ids=true, to_apply=%region_10.0 | all-reduce | flops 2400 | bytes 19200 | tf_op jit(solution)/shard_map/pmax | solution.py:78
  101.6 1.4 fusion.1
  103.0 0.6 stack.39
  103.6 0.9 fusion.3
  104.5 0.6 stack.40
  105.3 0.6 stack.41
  106.2 0.6 stack.42
  107.0 0.6 stack.43
  107.9 0.5 stack.44
  108.7 0.6 stack.45
  109.5 0.6 stack.46
  110.4 0.4 copy-done.12
  110.8 0.9 convolution_dynamic-update-slice_fusion.7
  111.7 0.9 convolution_dynamic-update-slice_fusion.6
  112.6 0.9 convolution_dynamic-update-slice_fusion.5
  113.5 0.9 convolution_dynamic-update-slice_fusion.4
  114.4 0.9 convolution_dynamic-update-slice_fusion.3
  115.3 0.9 convolution_dynamic-update-slice_fusion.2
  116.2 0.9 convolution_dynamic-update-slice_fusion.1
  117.2 0.9 convolution_dynamic-update-slice_fusion
  118.2 1.8 bitcast_multiply_fusion
  120.0 58.2 %psum.15 = f32[300,8]{0,1:T(8,128)S(1)} all-reduce(f32[300,8]{0,1:T(8,128)S(1)} %get-tuple-element.2), channel_id=1, replica_groups=mesh['scenes'=2,'rows'=4,'cols'=4] {'rows','cols'}, use_global_device_ids=true, to_apply=%region_20.0 | all-reduce | flops 2400 | bytes 19200 | tf_op jit(solution)/shard_map/psum | solution.py:80
  178.2 32.4 %all-reduce.2.cloned.1.call-done = f32[300,256]{0,1:T(8,128)} async-done(((f32[300,256]{0,1:T(8,128)}), f32[300,256]{0,1:T(8,128)}) %all-reduce.2.cloned.1.call-update) | async-done | bytes 307216 | tf_op jit(solution)/shard_map/psum | solution.py:80
  210.6 1.0 fusion.43
  212.2 0.9 subtract_multiply_fusion
  (79 shorter events, 4.6 us)
Async XLA Ops:
  7.2 25.6 %copy-start = (bf16[256,256]{1,0:T(8,128)(2,1)S(1)}, bf16[256,256]{1,0:T(8,128)(2,1)}, u32[]{:S(2)}) copy-start(bf16[256,256]{1,0:T(8,128)(2,1)} %param.15) | copy-start | bytes 393220
  7.2 5.5 %copy-start.9 = (bf16[256,256]{1,0:T(8,128)(2,1)S(1)}, bf16[256,256]{1,0:T(8,128)(2,1)}, u32[]{:S(2)}) copy-start(bf16[256,256]{1,0:T(8,128)(2,1)} %param.14) | copy-start | bytes 393220
  7.2 203.4 %all-reduce.2.cloned.1.call-start = ((), (), s32[]{:S(2)}) async-start(), calls=%async_computation | async-start | bytes 786432 | tf_op jit(solution)/shard_map/psum | solution.py:80
  8.0 6.0 %collective-permute-start = (bf16[3,16,256]{2,1,0:T(8,128)(2,1)S(1)}, bf16[3,16,256]{2,1,0:T(8,128)(2,1)S(1)}, u32[]{:S(2)}, u32[]{:S(2)}) collective-permute-start(bf16[3,16,256]{2,1,0:T(8,128)(2,1)S(1)} %get-tuple-element.12), channel_id=1, source_target_pairs={{0,4},{4,8},{8,12},{1,5},{5,9},{9,13},{2,6},{6,10},{10,14},{3,7},{... | collective-permute-start | bytes 73736 | tf_op jit(solution)/shard_map/ppermute | solution.py:16
  10.4 5.2 %collective-permute-start.1 = (bf16[3,16,256]{2,1,0:T(8,128)(2,1)S(1)}, bf16[3,16,256]{2,1,0:T(8,128)(2,1)S(1)}, u32[]{:S(2)}, u32[]{:S(2)}) collective-permute-start(bf16[3,16,256]{2,1,0:T(8,128)(2,1)S(1)} %get-tuple-element.11), channel_id=1, source_target_pairs={{4,0},{8,4},{12,8},{5,1},{9,5},{13,9},{6,2},{10,6},{14,10},{7,3},{... | collective-permute-start | bytes 73736 | tf_op jit(solution)/shard_map/ppermute | solution.py:17
  12.7 1.3 copy-start.10
  12.7 1.3 copy-start.4
  15.7 5.5 %collective-permute-start.2 = (bf16[38,3,256]{2,1,0:T(4,128)(2,1)S(1)}, bf16[38,3,256]{2,1,0:T(4,128)(2,1)S(1)}, u32[]{:S(2)}, u32[]{:S(2)}) collective-permute-start(bf16[38,3,256]{2,1,0:T(4,128)(2,1)S(1)} %get-tuple-element.6), channel_id=1, source_target_pairs={{0,1},{1,2},{2,3},{4,5},{5,6},{6,7},{8,9},{9,10},{10,11},{12,13},{... | collective-permute-start | bytes 175112 | tf_op jit(solution)/shard_map/ppermute | solution.py:16
  19.1 6.3 %collective-permute-start.3 = (bf16[38,3,256]{2,1,0:T(4,128)(2,1)S(1)}, bf16[38,3,256]{2,1,0:T(4,128)(2,1)S(1)}, u32[]{:S(2)}, u32[]{:S(2)}) collective-permute-start(bf16[38,3,256]{2,1,0:T(4,128)(2,1)S(1)} %get-tuple-element.7), channel_id=1, source_target_pairs={{1,0},{2,1},{3,2},{5,4},{6,5},{7,6},{9,8},{10,9},{11,10},{13,12},{... | collective-permute-start | bytes 175112 | tf_op jit(solution)/shard_map/ppermute | solution.py:17
  31.9 0.7 copy-start.23
  32.8 77.3 %copy-start.5 = (bf16[32,16,256]{2,1,0:T(8,128)(2,1)}, bf16[32,16,256]{2,1,0:T(8,128)(2,1)S(1)}, u32[]{:S(2)}) copy-start(bf16[32,16,256]{2,1,0:T(8,128)(2,1)S(1)} %fusion.42) | copy-start | bytes 786436
  34.1 4.1 %copy-start.11 = (f32[300]{0:T(512)}, f32[300]{0:T(512)S(1)}, u32[]{:S(2)}) copy-start(f32[300]{0:T(512)S(1)} %get-tuple-element.66) | copy-start | bytes 3604
  35.2 3.0 %copy-start.13 = (f32[300]{0:T(512)}, f32[300]{0:T(512)S(1)}, u32[]{:S(2)}) copy-start(f32[300]{0:T(512)S(1)} %get-tuple-element.68) | copy-start | bytes 3604
  101.5 2.0 copy-start.3
  101.5 3.5 %copy-start.1 = (f32[300,512]{1,0:T(8,128)S(1)}, f32[300,512]{1,0:T(8,128)}, u32[]{:S(2)}) copy-start(f32[300,512]{1,0:T(8,128)} %get-tuple-element.71) | copy-start | bytes 1843204
  108.4 1.7 copy-start.7
  109.2 1.1 copy-start.2
  110.1 0.7 copy-start.12
  110.8 0.9 copy-start.14
  117.1 1.0 copy-start.15
  117.1 1.0 copy-start.16
  117.2 1.0 copy-start.17
  117.2 1.0 copy-start.18
  117.2 1.0 copy-start.19
  117.2 1.0 copy-start.20
  117.2 1.0 copy-start.21
  117.2 1.0 copy-start.22
  178.2 33.4 %copy-start.6 = (bf16[300,256]{1,0:T(8,128)(2,1)S(1)}, bf16[300,256]{1,0:T(8,128)(2,1)}, u32[]{:S(2)}) copy-start(bf16[300,256]{1,0:T(8,128)(2,1)} %param.12) | copy-start | bytes 460804
  178.2 33.5 %copy-start.8 = (bf16[256,256]{1,0:T(8,128)(2,1)S(1)}, bf16[256,256]{1,0:T(8,128)(2,1)}, u32[]{:S(2)}) copy-start(bf16[256,256]{1,0:T(8,128)(2,1)} %param.17) | copy-start | bytes 393220
Sparse Core Ops, SparseCore 0:
  120.1 90.4 all-reduce.1
where the time goes:
time: 220 us
  blocking collectives  118 us (54%)
  waiting for transfers between devices  38.9 us (18%)
  matrix products  14.5 us (7%)
  other arithmetic  14.5 us (7%)
  between operations  14.4 us (7%)
  local copies, waits for them, and re-layouts  11.4 us (5%)
  starting transfers between devices  8.45 us (4%)
    pmax x1, blocking collectives, body(): global_max = lax.pmax(maxima, ('rows', 'cols'))  59.7 us
    psum x1, blocking collectives, body(): lax.psum((totals * rescale, sums * widen(rescale)), ('rows', 'cols'))  58.2 us
    psum x1, waiting for transfers between devices, body(): lax.psum((totals * rescale, sums * widen(rescale)), ('rows', 'cols'))  32.4 us
    dot_general x8, matrix products, body(): jnp.dot(expo.astype(jnp.bfloat16), values[:, low:low + head_dim], preferr...  7.25 us
    reduce_sum x1, other arithmetic, layer_norm(): centred = vector - jnp.mean(vector, axis=-1, keepdims=True)  6.16 us
    ppermute x2, starting transfers between devices, with_halo(): before = lax.ppermute(last, axis, up)  5.83 us
    ppermute x2, waiting for transfers between devices, with_halo(): after = lax.ppermute(initial, axis, down)  5.76 us
    dot_general x8, matrix products, body(): lax.dot_general(queries[:, low:low + head_dim], keys[:, low:low + head_di...  5.14 us
  transfers between devices with their start and end apart: 5, of which 4 were waited for; matrix products, arithmetic and copies ran while one was open for 1% of the time, Pallas kernels for 0%

commit v1 on v0

--- a/solution.py
+++ b/solution.py
@@ -77,7 +77,7 @@
 
     global_max = lax.pmax(maxima, ("rows", "cols"))
     rescale = jnp.exp(maxima - global_max)
-    totals, sums = lax.psum((totals * rescale, sums * widen(rescale)), ("rows", "cols"))
+    totals, sums = lax.psum(lax.psum((totals * rescale, sums * widen(rescale)), "cols"), "rows")
     attended = (sums / widen(totals)).astype(jnp.bfloat16)
     projected = jnp.dot(attended, w_out, preferred_element_type=jnp.float32)
     decoded = layer_norm(query_state.astype(jnp.float32) + projected)

time: 220 us -> 202 us (0.918)
  blocking collectives: 118 us -> 87.5 us
  waiting for transfers between devices: 38.9 us -> 50.4 us
    psum x1 -> x2, blocking collectives: 58.2 us -> 27.8 us  [the longest x1 17.3 us: body(): lax.psum((totals * rescale, sums * widen(rescale)), 'cols')]
    psum x1 -> x2, waiting for transfers between devices: 32.4 us -> 44 us  [the longest x1 37.1 us: body(): lax.psum((totals * rescale, sums * widen(rescale)), 'cols')]
  transfers between devices with their start and end apart: 5 -> 6, of which waited for: 4 -> 5; matrix products, arithmetic and copies ran while one was open for 1% -> 1% of each run, Pallas kernels for 0% -> 0%
where the time goes in v1:
time: 202 us; the launch traced here: 201 us
  blocking collectives  87.5 us (43%)
  waiting for transfers between devices  50.4 us (25%)
  matrix products  14.5 us (7%)
  other arithmetic  14.5 us (7%)
  between operations  14.4 us (7%)
  local copies, waits for them, and re-layouts  11.4 us (6%)
  starting transfers between devices  8.49 us (4%)
    pmax x1, blocking collectives, body(): global_max = lax.pmax(maxima, ('rows', 'cols'))  59.7 us
    psum x1, waiting for transfers between devices, body(): lax.psum((totals * rescale, sums * widen(rescale)), 'cols')  37.1 us
    psum x1, blocking collectives, body(): lax.psum((totals * rescale, sums * widen(rescale)), 'cols')  17.3 us
    psum x1, blocking collectives, body(): lax.psum(lax.psum((totals * rescale, sums * widen(rescale)), 'cols'), 'ro...  10.5 us
    dot_general x8, matrix products, body(): jnp.dot(expo.astype(jnp.bfloat16), values[:, low:low + head_dim], preferr...  7.25 us
    psum x1, waiting for transfers between devices, body(): lax.psum(lax.psum((totals * rescale, sums * widen(rescale)), 'cols'), 'ro...  6.85 us
    reduce_sum x1, other arithmetic, layer_norm(): centred = vector - jnp.mean(vector, axis=-1, keepdims=True)  6.16 us
    ppermute x2, starting transfers between devices, with_halo(): before = lax.ppermute(last, axis, up)  5.83 us
  transfers between devices with their start and end apart: 6, of which 5 were waited for; matrix products, arithmetic and copies ran while one was open for 1% of the time, Pallas kernels for 0%

profile of v1, /device:TPU:0, one launch (start us, length us, event | category | flops | bytes accessed | tf_op | source)
XLA Modules:
  0.0 201.2 jit_solution(5390886066636382096)
XLA Ops:
  7.2 0.8 fusion.138
  8.0 2.3 %collective-permute-start = (bf16[3,16,256]{2,1,0:T(8,128)(2,1)S(1)}, bf16[3,16,256]{2,1,0:T(8,128)(2,1)S(1)}, u32[]{:S(2)}, u32[]{:S(2)}) collective-permute-start(bf16[3,16,256]{2,1,0:T(8,128)(2,1)S(1)} %get-tuple-element.12), channel_id=1, source_target_pairs={{0,4},{4,8},{8,12},{1,5},{5,9},{9,13},{2,6},{6,10},{10,14},{3,7},{... | collective-permute-start | bytes 73736 | tf_op jit(solution)/shard_map/ppermute | solution.py:16
  10.4 1.3 collective-permute-start.1
  11.7 1.0 fusion.139
  12.7 1.2 fusion
  14.1 1.5 collective-permute-done.1
  15.7 3.5 %collective-permute-start.2 = (bf16[38,3,256]{2,1,0:T(4,128)(2,1)S(1)}, bf16[38,3,256]{2,1,0:T(4,128)(2,1)S(1)}, u32[]{:S(2)}, u32[]{:S(2)}) collective-permute-start(bf16[38,3,256]{2,1,0:T(4,128)(2,1)S(1)} %get-tuple-element.6), channel_id=1, source_target_pairs={{0,1},{1,2},{2,3},{4,5},{5,6},{6,7},{8,9},{9,10},{10,11},{12,13},{... | collective-permute-start | bytes 175112 | tf_op jit(solution)/shard_map/ppermute | solution.py:16
  19.1 1.3 collective-permute-start.3
  20.5 0.7 collective-permute-done.2
  21.1 4.3 %collective-permute-done.3 = bf16[38,3,256]{2,1,0:T(4,128)(2,1)S(1)} collective-permute-done((bf16[38,3,256]{2,1,0:T(4,128)(2,1)S(1)}, bf16[38,3,256]{2,1,0:T(4,128)(2,1)S(1)}, u32[]{:S(2)}, u32[]{:S(2)}) %collective-permute-start.3) | collective-permute-done | bytes 58400 | tf_op jit(solution)/shard_map/ppermute | solution.py:17
  25.4 6.2 %fusion.135 = (f32[32,16]{1,0:T(8,128)S(1)}, f32[32,16,256]{2,1,0:T(8,128)S(1)}) fusion(f32[256]{0:T(256)S(1)} %bitcast.113, bf16[38,3,256]{2,1,0:T(4,128)(2,1)S(1)} %collective-permute-done.3, bf16[38,16,256]{2,1,0:T(8,128)(2,1)S(1)} %get-tuple-element.65, f32[256]{0:T(256)S(1)} %bitcast.112, f32[256]{0:T(256)S(1)} %bitcast.111, f32[256]{0:T(256)S(1)} %bitcast.110, ...), kind=kLoop, calls=%fused_computation.248 | loop fusion | flops 35782144 | bytes 2839552 | tf_op jit(solution)/shard_map/reduce_sum | solution.py:23
  31.9 0.7 copy-done.23
  33.1 1.0 fusion.142
  34.1 1.1 fusion.143
  35.2 1.1 fusion.144
  38.3 0.6 broadcast_in_dim.38
  38.8 0.6 broadcast_in_dim.39
  39.4 0.6 broadcast_in_dim.40
  40.0 0.6 broadcast_in_dim.41
  40.6 0.6 broadcast_in_dim.42
  41.2 0.7 stack.38
  41.9 59.7 %pmax.7 = f32[300,8]{0,1:T(8,128)S(1)} all-reduce(f32[300,8]{0,1:T(8,128)S(1)} %stack.38), channel_id=1, replica_groups=mesh['scenes'=2,'rows'=4,'cols'=4] {'rows','cols'}, use_global_device_ids=true, to_apply=%region_10.0 | all-reduce | flops 2400 | bytes 19200 | tf_op jit(solution)/shard_map/pmax | solution.py:78
  101.6 1.4 fusion.1
  103.0 0.6 stack.39
  103.6 0.9 fusion.3
  104.5 0.6 stack.40
  105.3 0.6 stack.41
  106.2 0.6 stack.42
  107.0 0.6 stack.43
  107.9 0.5 stack.44
  108.7 0.6 stack.45
  109.5 0.6 stack.46
  110.4 0.4 copy-done.12
  110.8 0.9 convolution_dynamic-update-slice_fusion.7
  111.7 0.9 convolution_dynamic-update-slice_fusion.6
  112.6 0.9 convolution_dynamic-update-slice_fusion.5
  113.5 0.9 convolution_dynamic-update-slice_fusion.4
  114.4 0.9 convolution_dynamic-update-slice_fusion.3
  115.3 0.9 convolution_dynamic-update-slice_fusion.2
  116.2 0.9 convolution_dynamic-update-slice_fusion.1
  117.2 0.9 convolution_dynamic-update-slice_fusion
  118.2 1.8 bitcast_multiply_fusion
  120.1 37.1 %all-reduce.3.cloned.1.call-done = f32[300,256]{0,1:T(8,128)} async-done(((f32[300,256]{0,1:T(8,128)}), f32[300,256]{0,1:T(8,128)}) %all-reduce.3.cloned.1.call-update) | async-done | bytes 307216 | tf_op jit(solution)/shard_map/psum | solution.py:80
  157.2 17.3 %psum.30 = f32[300,8]{0,1:T(8,128)S(1)} all-reduce(f32[300,8]{0,1:T(8,128)S(1)} %get-tuple-element.2), channel_id=1, replica_groups=mesh['scenes'=2,'rows'=4,'cols'=4] {'cols'}, use_global_device_ids=true, to_apply=%region_21.0 | all-reduce | flops 2400 | bytes 19200 | tf_op jit(solution)/shard_map/psum | solution.py:80
  174.5 10.5 %psum.31 = f32[300,8]{0,1:T(8,128)S(1)} all-reduce(f32[300,8]{0,1:T(8,128)S(1)} %psum.30), channel_id=1, replica_groups=mesh['scenes'=2,'rows'=4,'cols'=4] {'rows'}, use_global_device_ids=true, to_apply=%region_22.0 | all-reduce | flops 2400 | bytes 19200 | tf_op jit(solution)/shard_map/psum | solution.py:80
  185.0 6.9 %all-reduce.5.cloned.1.call-done = f32[300,256]{0,1:T(8,128)} async-done(((f32[300,256]{0,1:T(8,128)}), f32[300,256]{0,1:T(8,128)}) %all-reduce.5.cloned.1.call-update) | async-done | bytes 307216 | tf_op jit(solution)/shard_map/psum | solution.py:80
  191.9 1.0 fusion.43
  193.5 0.9 subtract_multiply_fusion
  (83 shorter events, 5.4 us)
Async XLA Ops:
  7.2 25.6 %copy-start = (bf16[256,256]{1,0:T(8,128)(2,1)S(1)}, bf16[256,256]{1,0:T(8,128)(2,1)}, u32[]{:S(2)}) copy-start(bf16[256,256]{1,0:T(8,128)(2,1)} %param.15) | copy-start | bytes 393220
  7.2 5.5 %copy-start.9 = (bf16[256,256]{1,0:T(8,128)(2,1)S(1)}, bf16[256,256]{1,0:T(8,128)(2,1)}, u32[]{:S(2)}) copy-start(bf16[256,256]{1,0:T(8,128)(2,1)} %param.14) | copy-start | bytes 393220
  7.2 150.0 %all-reduce.3.cloned.1.call-start = ((), (), s32[]{:S(2)}) async-start(), calls=%async_computation | async-start | bytes 786432 | tf_op jit(solution)/shard_map/psum | solution.py:80
  8.0 6.0 %collective-permute-start = (bf16[3,16,256]{2,1,0:T(8,128)(2,1)S(1)}, bf16[3,16,256]{2,1,0:T(8,128)(2,1)S(1)}, u32[]{:S(2)}, u32[]{:S(2)}) collective-permute-start(bf16[3,16,256]{2,1,0:T(8,128)(2,1)S(1)} %get-tuple-element.12), channel_id=1, source_target_pairs={{0,4},{4,8},{8,12},{1,5},{5,9},{9,13},{2,6},{6,10},{10,14},{3,7},{... | collective-permute-start | bytes 73736 | tf_op jit(solution)/shard_map/ppermute | solution.py:16
  10.4 5.2 %collective-permute-start.1 = (bf16[3,16,256]{2,1,0:T(8,128)(2,1)S(1)}, bf16[3,16,256]{2,1,0:T(8,128)(2,1)S(1)}, u32[]{:S(2)}, u32[]{:S(2)}) collective-permute-start(bf16[3,16,256]{2,1,0:T(8,128)(2,1)S(1)} %get-tuple-element.11), channel_id=1, source_target_pairs={{4,0},{8,4},{12,8},{5,1},{9,5},{13,9},{6,2},{10,6},{14,10},{7,3},{... | collective-permute-start | bytes 73736 | tf_op jit(solution)/shard_map/ppermute | solution.py:17
  12.7 1.3 copy-start.10
  12.7 1.3 copy-start.4
  15.7 5.5 %collective-permute-start.2 = (bf16[38,3,256]{2,1,0:T(4,128)(2,1)S(1)}, bf16[38,3,256]{2,1,0:T(4,128)(2,1)S(1)}, u32[]{:S(2)}, u32[]{:S(2)}) collective-permute-start(bf16[38,3,256]{2,1,0:T(4,128)(2,1)S(1)} %get-tuple-element.6), channel_id=1, source_target_pairs={{0,1},{1,2},{2,3},{4,5},{5,6},{6,7},{8,9},{9,10},{10,11},{12,13},{... | collective-permute-start | bytes 175112 | tf_op jit(solution)/shard_map/ppermute | solution.py:16
  19.1 6.3 %collective-permute-start.3 = (bf16[38,3,256]{2,1,0:T(4,128)(2,1)S(1)}, bf16[38,3,256]{2,1,0:T(4,128)(2,1)S(1)}, u32[]{:S(2)}, u32[]{:S(2)}) collective-permute-start(bf16[38,3,256]{2,1,0:T(4,128)(2,1)S(1)} %get-tuple-element.7), channel_id=1, source_target_pairs={{1,0},{2,1},{3,2},{5,4},{6,5},{7,6},{9,8},{10,9},{11,10},{13,12},{... | collective-permute-start | bytes 175112 | tf_op jit(solution)/shard_map/ppermute | solution.py:17
  31.9 0.7 copy-start.23
  32.8 77.3 %copy-start.5 = (bf16[32,16,256]{2,1,0:T(8,128)(2,1)}, bf16[32,16,256]{2,1,0:T(8,128)(2,1)S(1)}, u32[]{:S(2)}) copy-start(bf16[32,16,256]{2,1,0:T(8,128)(2,1)S(1)} %fusion.42) | copy-start | bytes 786436
  34.1 4.1 %copy-start.11 = (f32[300]{0:T(512)}, f32[300]{0:T(512)S(1)}, u32[]{:S(2)}) copy-start(f32[300]{0:T(512)S(1)} %get-tuple-element.66) | copy-start | bytes 3604
  35.2 3.0 %copy-start.13 = (f32[300]{0:T(512)}, f32[300]{0:T(512)S(1)}, u32[]{:S(2)}) copy-start(f32[300]{0:T(512)S(1)} %get-tuple-element.68) | copy-start | bytes 3604
  101.5 2.0 %copy-start.3 = (f32[300,512]{1,0:T(8,128)S(1)}, f32[300,512]{1,0:T(8,128)}, u32[]{:S(2)}) copy-start(f32[300,512]{1,0:T(8,128)} %get-tuple-element.69) | copy-start | bytes 1843204
  101.5 3.5 %copy-start.1 = (f32[300,512]{1,0:T(8,128)S(1)}, f32[300,512]{1,0:T(8,128)}, u32[]{:S(2)}) copy-start(f32[300,512]{1,0:T(8,128)} %get-tuple-element.71) | copy-start | bytes 1843204
  108.4 1.7 copy-start.7
  109.2 1.1 copy-start.2
  110.1 0.7 copy-start.12
  110.8 0.9 copy-start.14
  117.1 1.0 copy-start.15
  117.1 1.0 copy-start.16
  117.2 1.0 copy-start.17
  117.2 1.0 copy-start.18
  117.2 1.0 copy-start.19
  117.2 1.0 copy-start.20
  117.2 1.0 copy-start.21
  117.2 1.0 copy-start.22
  120.0 71.9 %all-reduce.5.cloned.1.call-start = ((), (), s32[]{:S(2)}) async-start(), calls=%async_computation.1 | async-start | bytes 786432 | tf_op jit(solution)/shard_map/psum | solution.py:80
  185.0 7.9 %copy-start.6 = (bf16[300,256]{1,0:T(8,128)(2,1)S(1)}, bf16[300,256]{1,0:T(8,128)(2,1)}, u32[]{:S(2)}) copy-start(bf16[300,256]{1,0:T(8,128)(2,1)} %param.12) | copy-start | bytes 460804
  185.0 7.9 %copy-start.8 = (bf16[256,256]{1,0:T(8,128)(2,1)S(1)}, bf16[256,256]{1,0:T(8,128)(2,1)}, u32[]{:S(2)}) copy-start(bf16[256,256]{1,0:T(8,128)(2,1)} %param.17) | copy-start | bytes 393220
Sparse Core Ops, SparseCore 0:
  120.1 36.9 all-reduce.2
  159.6 32.1 all-reduce.4
